TPU v7x, 256 devices: a whole 4x4x8 slice. The times are simulated.
256 devices in a mesh: ctx: 32 (over x, z), head: 8 (over y, core).
Axes of the slice: x: 4, y: 4, z: 8, core: 2. Of those that a mesh axis runs over, the one named last changes fastest.
Arguments:
- inputs: bfloat16 [16384, 8192], P(('ctx', 'head')), may hold values from -1.75 to 1.75
- grad_out: bfloat16 [16384, 8192], P(('ctx', 'head')), may hold values from -1.75 to 1.75
- steps: bfloat16 [16384, 128], P(('ctx', 'head')), may hold values from 0.049804688 to 0.19921875
- log_decay: bfloat16 [16384, 128], P(('ctx', 'head')), may hold values from -0.52 to 0
- input_map: bfloat16 [16384, 128], P(('ctx', 'head')), may hold values from -0.5 to 0.5
- output_map: bfloat16 [16384, 128], P(('ctx', 'head')), may hold values from -0.5 to 0.5
- skip_gain: float32 [128], P('head'), may hold values from 0.5 to 1.5
Outputs:
- grad_inputs: bfloat16 [16384, 8192], P(('ctx', 'head'))
- grad_steps: bfloat16 [16384, 128], P(('ctx', 'head'))
- grad_decay: bfloat16 [16384, 128], P(('ctx', 'head'))
- grad_input_map: float32 [16384, 128], P(('ctx', 'head'))
- grad_output_map: float32 [16384, 128], P(('ctx', 'head'))
All inputs are finite; a program needn't handle non-finite values.
Results may differ from a plain program's by a relative error of at most 0.004.
Values may be sent and summed in bfloat16 or wider, within the bound.
A program may use at most 128 MiB of HBM per device.

v0:
```python
import jax
import jax.numpy as jnp
from jax import lax
from jax.experimental import pallas as pl
from jax.experimental.pallas import tpu as pltpu
from jax.sharding import PartitionSpec as P

BF = jnp.bfloat16
F32 = jnp.float32
MESH = pl.DeviceIdType.MESH
NC = 32
NH = 8
TOK = 64
LEN = 512
Q = 128
CH = LEN // Q
W = 1024
HD = 64
N = 128
GH = 16
RB = 32
SOUT = F32
SBACK = BF
GOUT = BF
GBACK = BF

NN = ((1,), (0,))
NT = ((1,), (1,))


def dot(a, b, dims=NN):
    return lax.dot_general(a, b, (dims, ((), ())), preferred_element_type=F32)


def halves(a):
    hi = a.astype(BF)
    return hi, (a - hi.astype(F32)).astype(BF)


def iota(shape, axis):
    return lax.broadcasted_iota(jnp.int32, shape, axis)


def ones_where(cond):
    return jnp.where(cond, 1.0, 0.0).astype(BF)


def kernel(
    x, g, st, ld, bm, cm, skip, ox, ods, odq, ogb, ogc,
    gb, xb, sm, rep, f1, f2, f1d, f2d, rowf, tri, stc, cumc, ct2, bt2, gx, xs,
    lg, ls, acc, v, dxb, gin, sin, dec, decr, gs, gr, gbs, gbr, ss, sr, sbs, sbr,
    cs, rs, prod, gbp, gcp, gbrv, gcrv, pk, pkr, send, recv,
):
    me_c = lax.axis_index("ctx")
    me_h = lax.axis_index("head")

    def cpeer(r):
        return lax.rem(me_c + r, NC)

    def hpeer(r):
        return lax.rem(me_h + r, NH)

    def remote(src, dst, s, axis, to):
        pltpu.make_async_remote_copy(
            src_ref=src, dst_ref=dst, send_sem=send.at[s], recv_sem=recv.at[s],
            device_id={axis: to}, device_id_type=MESH,
        ).start()

    def local(src, dst, s):
        pltpu.make_async_copy(src, dst, recv.at[s]).start()

    def arrived(ref, s):
        pltpu.make_async_copy(ref, ref, recv.at[s]).wait()

    def left(ref, s):
        pltpu.make_async_copy(ref, ref, send.at[s]).wait()

    barrier = pltpu.get_barrier_semaphore()

    def greet_head(r, z):
        pl.semaphore_signal(barrier, inc=1, device_id={"head": hpeer(r)}, device_id_type=MESH)
        return z

    def greet_ctx(r, z):
        pl.semaphore_signal(barrier, inc=1, device_id={"ctx": cpeer(r)}, device_id_type=MESH)
        return z

    lax.fori_loop(1, NH, greet_head, 0)
    lax.fori_loop(1, NC, greet_ctx, 0)
    pl.semaphore_wait(barrier, NH + NC - 2)

    mine = pl.ds(pl.multiple_of(me_h * TOK, TOK), TOK)

    def cols(k):
        return pl.ds(pl.multiple_of(k * W, W), W)

    def send_small(r, z):
        to = hpeer(r)
        for a, src in enumerate((bm, cm, st, ld)):
            remote(src, sm.at[a, mine, :], 0, "head", to)
        return z

    def send_g(r, z):
        to = hpeer(r)
        remote(g.at[:, cols(to)], gb.at[mine, :], 1, "head", to)
        return z

    def send_x(r, z):
        to = hpeer(r)
        remote(x.at[:, cols(to)], xb.at[mine, :], 2, "head", to)
        return z

    lax.fori_loop(1, NH, send_small, 0)
    for a, src in enumerate((bm, cm, st, ld)):
        local(src, sm.at[a, mine, :], 0)
    lax.fori_loop(1, NH, send_g, 0)
    local(g.at[:, cols(me_h)], gb.at[mine, :], 1)
    lax.fori_loop(1, NH, send_x, 0)
    local(x.at[:, cols(me_h)], xb.at[mine, :], 2)

    rep_one = ones_where(iota((N, W), 0) == iota((N, W), 1) // HD)
    rep[0:N, :] = rep_one
    rep[N : 2 * N, :] = rep_one
    row, col = iota((Q, Q), 0), iota((Q, Q), 1)
    tri[...] = ones_where(row >= col)
    below = row >= col
    above = row <= col
    pick = ones_where((row == me_h * GH + col) & (col < GH))

    arrived(sm, 0)

    stc[...] = dot(sm[2], pick)
    lds = dot(sm[3], pick).astype(BF)
    tots = []
    for c in range(CH):
        cum = dot(tri[...], lds[c * Q : (c + 1) * Q, :])
        cumc[c * Q : (c + 1) * Q, :] = cum
        tots.append(cum[Q - 1 : Q, :])
    upto = [tots[0]]
    for c in range(1, CH):
        upto.append(upto[-1] + tots[c])
    beyond = [None] * CH
    beyond[CH - 1] = jnp.zeros_like(tots[0])
    for c in range(CH - 2, -1, -1):
        beyond[c] = beyond[c + 1] + tots[c + 1]
    for k in range(CH):
        prod[k : k + 1, 0:N] = tots[k]
        prod[CH + k : CH + k + 1, 0:N] = upto[k]
        prod[2 * CH + k : 2 * CH + k + 1, 0:N] = beyond[k]
        prod[3 * CH + k : 3 * CH + k + 1, 0:N] = jnp.zeros_like(tots[0])
    rows = jnp.exp(prod[:, 0:N])
    hi, rest = rows.astype(BF), rows - rows.astype(BF).astype(F32)
    mid, low = halves(rest)
    rowf[...] = dot(jnp.concatenate([hi, mid], axis=1), rep[...]) + dot(low, rep[0:N, :])
    dec[...] = jnp.broadcast_to(rowf[2 * CH - 1 : 2 * CH, :], (8, W))

    def send_decay(r, z):
        k = cpeer(r)
        remote(dec.at[:, pl.ds(pl.multiple_of(k // 4 * N, N), N)], decr.at[me_c], 3, "ctx", k)
        return z

    lax.fori_loop(1, NC, send_decay, 0)
    local(dec.at[:, pl.ds(pl.multiple_of(me_c // 4 * N, N), N)], decr.at[me_c], 3)

    def chunk(c):
        return pl.ds(pl.multiple_of(c * Q, Q), Q)

    def expand(a):
        return dot(jnp.concatenate(halves(a), axis=1), rep[...])

    def transposed(a, out, c):
        t = jnp.transpose(a.astype(F32)).astype(BF)
        out[c, :, 0:Q] = t
        out[c, :, Q : 2 * Q] = t

    for c in range(CH):
        at = slice(c * Q, (c + 1) * Q)
        cum = cumc[at, :]
        s = stc[at, :]
        f1[at, :] = expand(jnp.exp(cum))
        f2[at, :] = expand(s * jnp.exp(-cum))
        f1d[at, :] = expand(jnp.exp(cum + (upto[c] - tots[c])))
        f2d[at, :] = expand(s * jnp.exp(tots[c] - cum + beyond[c]))
        transposed(sm[0, at, :], bt2, c)
        transposed(sm[1, at, :], ct2, c)
    skip_hi = skip[...].astype(BF)
    skip_rest = skip[...] - skip_hi.astype(F32)
    skip_mid, skip_low = halves(skip_rest)
    skip_row = (
        dot(skip_hi, rep[0:GH, :]) + dot(skip_mid, rep[0:GH, :]) + dot(skip_low, rep[0:GH, :])
    )

    arrived(gb, 1)
    acc[...] = jnp.zeros_like(acc)

    def step_g(r, z):
        c = CH - 1 - r
        at = chunk(c)
        ghi, glo = halves(gb[at, :].astype(F32) * f1[at, :])
        gx[c, 0:Q, :] = ghi
        end = acc[...]
        lg[c] = end
        end = end * rowf[pl.ds(c, 1), :]
        gx[c, Q : 2 * Q, :] = end.astype(BF)
        acc[...] = end + dot(ct2[c], jnp.concatenate([ghi, glo], axis=0))
        return z

    lax.fori_loop(0, CH, step_g, 0)

    def stage(src, dst):
        for k in range(NC):
            a, b = k % 4 * RB, k // 4 * N
            dst[k] = src[a : a + RB, b : b + N].astype(dst.dtype)

    def unstage(src, dst):
        for k in range(NC):
            a, b = k % 4 * RB, k // 4 * N
            dst[a : a + RB, b : b + N] = src[k].astype(dst.dtype)

    def spread(src, dst, s):
        def one(r, z):
            k = cpeer(r)
            remote(src.at[k], dst.at[me_c], s, "ctx", k)
            return z

        lax.fori_loop(1, NC, one, 0)
        local(src.at[me_c], dst.at[me_c], s)

    stage(acc, gs)
    spread(gs, gr, 4)

    def step_u(c, z):
        at = chunk(c)
        b = sm[0, at, :]
        cb = jnp.where(above, dot(b, sm[1, at, :], NT), 0.0).astype(BF)
        v[at, :] = f2[at, :] * dot(jnp.concatenate([cb, b], axis=1), gx[c])
        return z

    lax.fori_loop(0, CH, step_u, 0)

    arrived(decr, 3)
    arrived(gr, 4)

    def back_g(r, carry):
        i = NC - 1 - r
        gbs[i] = carry.astype(gbs.dtype)
        return carry * decr[i][0:1, :] + gr[i].astype(F32)

    lax.fori_loop(0, NC, back_g, jnp.zeros((RB, N), F32))
    spread(gbs, gbr, 5)

    arrived(xb, 2)
    acc[...] = jnp.zeros_like(acc)

    def step_x(c, z):
        at = chunk(c)
        xhi, xlo = halves(xb[at, :].astype(F32) * f2[at, :])
        xs[c, 0:Q, :] = xhi
        start = acc[...]
        ls[c] = start
        xs[c, Q : 2 * Q, :] = start.astype(BF)
        more = dot(bt2[c], jnp.concatenate([xhi, xlo], axis=0))
        acc[...] = (start + more) * rowf[pl.ds(c, 1), :]
        return z

    lax.fori_loop(0, CH, step_x, 0)
    ls[CH] = acc[...]
    stage(acc, ss)
    spread(ss, sr, 6)

    arrived(gbr, 5)
    unstage(gbr, gin)

    def block(k):
        return pl.ds(pl.multiple_of(k * TOK, TOK), TOK)

    def make_dx(p):
        at = chunk(p)
        now = v[at, :] + f2d[at, :] * dot(sm[0, at, :], gin[...])
        v[at, :] = now
        dxb[at, :] = (now + skip_row * gb[at, :].astype(F32)).astype(BF)

    def send_dx(to):
        remote(dxb.at[block(to), :], ox.at[:, cols(me_h)], 7, "head", to)

    def step_dx(r, z):
        p = lax.rem(me_h // 2 + r, NH // 2)
        make_dx(p)
        send_dx(2 * p)
        send_dx(2 * p + 1)
        return z

    lax.fori_loop(1, NH // 2, step_dx, 0)
    make_dx(me_h // 2)
    send_dx(me_h + 1 - 2 * lax.rem(me_h, 2))
    local(dxb.at[block(me_h), :], ox.at[:, cols(me_h)], 7)

    arrived(sr, 6)

    def back_s(i, carry):
        sbs[i] = carry.astype(sbs.dtype)
        return carry * decr[i][0:1, :] + sr[i].astype(F32)

    lax.fori_loop(0, NC, back_s, jnp.zeros((RB, N), F32))
    spread(sbs, sbr, 8)

    def heads_sum(a):
        hi, lo = halves(a)
        return dot(hi, rep[0:N, :], NT) + dot(lo, rep[0:N, :], NT)

    def step_local(c, z):
        at = chunk(c)
        b, cc = sm[0, at, :], sm[1, at, :]
        gh, xh = gx[c, 0:Q, :], xs[c, 0:Q, :]
        xf, gf = xb[at, :].astype(F32), gb[at, :].astype(F32)
        cs[at, :] = heads_sum(xf * v[at, :])
        e = jnp.where(below, dot(gh, xh, NT), 0.0).astype(BF)
        et = jnp.where(above, dot(xh, gh, NT), 0.0).astype(BF)
        gbp[at, :] = (
            dot(et, cc)
            + dot(xh, gx[c, Q : 2 * Q, :], NT)
            + dot((xf * f2d[at, :]).astype(BF), gin[...], NT)
        )
        gcp[at, :] = dot(e, b) + dot(gh, xs[c, Q : 2 * Q, :], NT)
        cb = jnp.where(below, dot(cc, b, NT), 0.0).astype(BF)
        y = f1[at, :] * dot(jnp.concatenate([cb, cc], axis=1), xs[c])
        rs[at, :] = heads_sum(gf * y)
        return z

    lax.fori_loop(0, CH, step_local, 0)

    def share(src, dst, s):
        def one(r, z):
            to = hpeer(r)
            remote(src.at[block(to), :], dst.at[me_h], s, "head", to)
            return z

        lax.fori_loop(1, NH, one, 0)
        local(src.at[block(me_h), :], dst.at[me_h], s)

    share(gbp, gbrv, 9)

    arrived(sbr, 8)
    unstage(sbr, sin)

    def step_s(c, z):
        at = chunk(c)
        gf = gb[at, :].astype(F32)
        gd = gf * f1d[at, :]
        gcp[at, :] = gcp[at, :] + dot(gd.astype(BF), sin[...], NT)
        rs[at, :] = rs[at, :] + heads_sum(gd * dot(sm[1, at, :], sin[...]))
        return z

    lax.fori_loop(0, CH, step_s, 0)
    share(gcp, gcrv, 10)

    prod[...] = jnp.zeros_like(prod)
    for c in range(CH):
        ge = lg[c] + rowf[2 * CH + c : 2 * CH + c + 1, :] * gin[...].astype(F32)
        se = ls[c + 1] + rowf[CH + c : CH + c + 1, :] * sin[...].astype(F32)
        prod[c : c + 1, :] = jnp.sum(ge * se, axis=0, keepdims=True)
    base = heads_sum(prod[...])
    lane = iota((Q, N), 1)
    upper = ones_where(above)
    for c in range(CH):
        at = slice(c * Q, (c + 1) * Q)
        csum = cs[at, :]
        hi, lo = halves(rs[at, :] - csum)
        dq = base[c : c + 1, :] + dot(upper, hi) + dot(upper, lo)
        ds = jnp.where(lane < GH, csum / jnp.where(lane < GH, stc[at, :], 1.0), 0.0)
        pk[at, :] = (ds + pltpu.roll(dq, GH, 1)).astype(BF)

    def send_pk(r, z):
        to = hpeer(r)
        remote(pk.at[block(to), :], pkr.at[:, pl.ds(pl.multiple_of(me_h * N, N), N)], 11, "head", to)
        return z

    lax.fori_loop(1, NH, send_pk, 0)
    local(pk.at[block(me_h), :], pkr.at[:, pl.ds(pl.multiple_of(me_h * N, N), N)], 11)

    arrived(gbrv, 9)
    ogb[...] = jnp.sum(gbrv[...], axis=0)
    arrived(gcrv, 10)
    ogc[...] = jnp.sum(gcrv[...], axis=0)
    arrived(pkr, 11)
    a, b = iota((W, N), 0), iota((W, N), 1)
    want = b // GH * N + b - b // GH * GH
    ods[...] = dot(pkr[...], ones_where(a == want)).astype(BF)
    odq[...] = dot(pkr[...], ones_where(a == want + GH)).astype(BF)
    arrived(ox, 7)

    left(sm.at[:, pl.ds(0, LEN - TOK), :], 0)
    left(gb.at[pl.ds(0, LEN - TOK), :], 1)
    left(xb.at[pl.ds(0, LEN - TOK), :], 2)
    left(decr.at[pl.ds(0, NC - 1)], 3)
    left(gs.at[pl.ds(0, NC - 1)], 4)
    left(gbs.at[pl.ds(0, NC - 1)], 5)
    left(ss.at[pl.ds(0, NC - 1)], 6)
    left(dxb.at[pl.ds(0, LEN - TOK), :], 7)
    left(sbs.at[pl.ds(0, NC - 1)], 8)
    left(gbp.at[pl.ds(0, LEN - TOK), :], 9)
    left(gcp.at[pl.ds(0, LEN - TOK), :], 10)
    left(pk.at[pl.ds(0, LEN - TOK), :], 11)


def body(inputs, grad_out, steps, log_decay, input_map, output_map, skip_gain):
    hbm = pl.BlockSpec(memory_space=pl.ANY)
    vmem = pl.BlockSpec(memory_space=pltpu.VMEM)

    def vm(shape, kind):
        return pltpu.VMEM(shape, kind)

    grads = pl.pallas_call(
        kernel,
        out_shape=(
            jax.ShapeDtypeStruct((TOK, NH * W), BF),
            jax.ShapeDtypeStruct((TOK, N), BF),
            jax.ShapeDtypeStruct((TOK, N), BF),
            jax.ShapeDtypeStruct((TOK, N), F32),
            jax.ShapeDtypeStruct((TOK, N), F32),
        ),
        in_specs=[hbm] * 6 + [vmem],
        out_specs=(hbm, vmem, vmem, vmem, vmem),
        scratch_shapes=[
            vm((LEN, W), BF),
            vm((LEN, W), BF),
            vm((4, LEN, N), BF),
            vm((2 * N, W), BF),
            vm((LEN, W), F32),
            vm((LEN, W), F32),
            vm((LEN, W), F32),
            vm((LEN, W), F32),
            vm((4 * CH, W), F32),
            vm((Q, Q), BF),
            vm((LEN, N), F32),
            vm((LEN, N), F32),
            vm((CH, N, 2 * Q), BF),
            vm((CH, N, 2 * Q), BF),
            vm((CH, 2 * Q, W), BF),
            vm((CH, 2 * Q, W), BF),
            vm((CH, N, W), F32),
            vm((CH + 1, N, W), F32),
            vm((N, W), F32),
            vm((LEN, W), F32),
            vm((LEN, W), BF),
            vm((N, W), BF),
            vm((N, W), BF),
            vm((8, W), F32),
            vm((NC, 8, N), F32),
            vm((NC, RB, N), GOUT),
            vm((NC, RB, N), GOUT),
            vm((NC, RB, N), GBACK),
            vm((NC, RB, N), GBACK),
            vm((NC, RB, N), SOUT),
            vm((NC, RB, N), SOUT),
            vm((NC, RB, N), SBACK),
            vm((NC, RB, N), SBACK),
            vm((LEN, N), F32),
            vm((LEN, N), F32),
            vm((4 * CH, W), F32),
            vm((LEN, N), F32),
            vm((LEN, N), F32),
            vm((NH, TOK, N), F32),
            vm((NH, TOK, N), F32),
            vm((LEN, N), BF),
            vm((TOK, NH * N), BF),
            pltpu.SemaphoreType.DMA((12,)),
            pltpu.SemaphoreType.DMA((12,)),
        ],
        compiler_params=pltpu.CompilerParams(
            collective_id=0, has_side_effects=True, vmem_limit_bytes=56 * 1024 * 1024
        ),
        cost_estimate=pl.CostEstimate(
            flops=3 * 10**9, bytes_accessed=8 * 2**20, transcendentals=2**20
        ),
        name="block_backward",
    )(inputs, grad_out, steps, log_decay, input_map, output_map, skip_gain.reshape(1, GH))
    return grads


def solution(mesh):
    spread = P(("ctx", "head"), None)
    return jax.shard_map(
        body,
        mesh=mesh,
        in_specs=(spread,) * 6 + (P("head"),),
        out_specs=(spread,) * 5,
        check_vma=False,
    )
```

profile of v0, /device:TPU:1, one launch (start us, length us, event | category | flops | bytes accessed | tf_op | source)
XLA Modules:
  0.0 83.0 jit_solution(3417050037559247396)
XLA Ops:
  0.6 77.4 %block_backward.1 = (bf16[64,8192]{1,0:T(8,128)(2,1)}, bf16[64,128]{1,0:T(8,128)(2,1)}, bf16[64,128]{1,0:T(8,128)(2,1)}, f32[64,128]{1,0:T(8,128)}, f32[64,128]{1,0:T(8,128)}) custom-call(bf16[64,8192]{1,0:T(8,128)(2,1)} %x.1, bf16[64,8192]{1,0:T(8,128)(2,1)} %g.1, bf16[64,128]{1,0:T(8,128)(2,1)} %st.1, bf16[64,128]{1,0:T(8,128)(2,1)} %ld.1, ...), custom_call_target="tpu_custom_call" | custom-call | flops 3000000000 | bytes 8388608 | tf_op jit(solution)/shard_map/block_backward/pallas_call | solution.py:413
  78.1 0.0 copy-start.3
  78.1 0.0 copy-start.2
  78.1 2.3 %copy.17 = bf16[64,8192]{1,0:T(8,128)(2,1)} copy(bf16[64,8192]{1,0:T(8,128)(2,1)} %get-tuple-element.10) | data formatting | bytes 2097152
  80.4 0.0 copy-done.3
  80.4 0.0 copy-start.1
  80.4 0.6 copy.18
  81.0 0.0 copy-done.2
  81.0 0.6 copy.19
  81.6 0.0 copy-done.1
  81.6 0.0 copy-start
  81.6 0.6 copy.20
  82.2 0.2 copy-done
  82.4 0.6 copy.21
Async XLA Ops:
  78.1 2.3 %copy-start.3 = (bf16[64,128]{1,0:T(8,128)(2,1)S(1)}, bf16[64,128]{1,0:T(8,128)(2,1)}, u32[]{:S(2)}) copy-start(bf16[64,128]{1,0:T(8,128)(2,1)} %get-tuple-element.11) | copy-start | bytes 49156
  78.1 2.9 %copy-start.2 = (bf16[64,128]{1,0:T(8,128)(2,1)S(1)}, bf16[64,128]{1,0:T(8,128)(2,1)}, u32[]{:S(2)}) copy-start(bf16[64,128]{1,0:T(8,128)(2,1)} %get-tuple-element.12) | copy-start | bytes 49156
  80.4 1.2 %copy-start.1 = (f32[64,128]{1,0:T(8,128)S(1)}, f32[64,128]{1,0:T(8,128)}, u32[]{:S(2)}) copy-start(f32[64,128]{1,0:T(8,128)} %get-tuple-element.13) | copy-start | bytes 98308
  81.6 0.8 copy-start
where the time goes:
time: 83.2 us; the launch traced here: 83 us
  Pallas kernels  77.4 us (93%)
  local copies, waits for them, and re-layouts  4.88 us (6%)
    pallas_call x1, Pallas kernels, body(): pl.pallas_call(kernel, out_shape=(jax.ShapeDtypeStruct((TOK, NH * W), BF)...  77.4 us
    unnamed x13, local copies, waits for them, and re-layouts  4.88 us

commit v1 on v0

v1 whole, which is shorter than its diff:
```python
import jax
import jax.numpy as jnp
from jax import lax
from jax.experimental import pallas as pl
from jax.experimental.pallas import tpu as pltpu
from jax.sharding import PartitionSpec as P

BF = jnp.bfloat16
F32 = jnp.float32
MESH = pl.DeviceIdType.MESH
NC = 32
NH = 8
TOK = 64
LEN = 512
Q = 128
CH = LEN // Q
W = 1024
HD = 64
N = 128
GH = 16
HW = W // 2
RB = 16
RG = N // RB
LG = HW // N
CHIPS = NH // 2

NN = ((1,), (0,))
NT = ((1,), (1,))


def dot(a, b, dims=NN):
    return lax.dot_general(a, b, (dims, ((), ())), preferred_element_type=F32)


def halves(a):
    hi = a.astype(BF)
    return hi, (a - hi.astype(F32)).astype(BF)


def iota(shape, axis):
    return lax.broadcasted_iota(jnp.int32, shape, axis)


def ones_where(cond):
    return jnp.where(cond, 1.0, 0.0).astype(BF)


def kernel(
    x, g, st, ld, bm, cm, skip, ox, ods, odq, ogb, ogc,
    gb, xb, sm, own, pki, pkr, rep, f1, f2, f1d, f2d, rowf, tri, stc, cumc, ct2, bt2, gx, xs,
    lg, ls, acc, v, dxb, gin, sin, dec, decr, gs, gr, gbs, gbr, gf32, ss, sr, sbs, sbr, pairs, pairr,
    cs, rs, prod, gbp, gcp, gbo, gco, gbh, gch, gbrv, gcrv, pko, pkv, send, recv,
):
    me_c = lax.axis_index("ctx")
    me_h = lax.axis_index("head")
    core = lax.rem(me_h, 2)
    chip = me_h // 2
    sibling = me_h + 1 - 2 * core

    def cpeer(r):
        return lax.rem(me_c + r, NC)

    def hpeer(r):
        return lax.rem(me_h + r, NH)

    def remote(src, dst, s, axis, to):
        pltpu.make_async_remote_copy(
            src_ref=src, dst_ref=dst, send_sem=send.at[s], recv_sem=recv.at[s],
            device_id={axis: to}, device_id_type=MESH,
        ).start()

    def local(src, dst, s):
        pltpu.make_async_copy(src, dst, recv.at[s]).start()

    def arrived(ref, s):
        pltpu.make_async_copy(ref, ref, recv.at[s]).wait()

    def left(ref, s):
        pltpu.make_async_copy(ref, ref, send.at[s]).wait()

    def block(k):
        return pl.ds(pl.multiple_of(k * TOK, TOK), TOK)

    def heads(k):
        return pl.ds(pl.multiple_of(k * GH, GH), GH)

    barrier = pltpu.get_barrier_semaphore()

    def greet_head(r, z):
        pl.semaphore_signal(barrier, inc=1, device_id={"head": hpeer(r)}, device_id_type=MESH)
        return z

    def greet_ctx(r, z):
        pl.semaphore_signal(barrier, inc=1, device_id={"ctx": cpeer(r)}, device_id_type=MESH)
        return z

    lax.fori_loop(1, NH, greet_head, 0)
    lax.fori_loop(1, NC, greet_ctx, 0)

    local(st, own.at[pl.ds(0, TOK), :], 24)
    local(ld, own.at[pl.ds(TOK, TOK), :], 24)
    rep_one = ones_where(iota((N, W), 0) == iota((N, W), 1) // HD)
    rep[0:N, :] = rep_one
    rep[N : 2 * N, :] = rep_one
    row, col = iota((Q, Q), 0), iota((Q, Q), 1)
    tri[...] = ones_where(row >= col)
    below = row >= col
    above = row <= col
    skip_hi = skip[...].astype(BF)
    skip_mid, skip_low = halves(skip[...] - skip_hi.astype(F32))
    skip_row = (
        dot(skip_hi, rep[0:GH, :]) + dot(skip_mid, rep[0:GH, :]) + dot(skip_low, rep[0:GH, :])
    )
    arrived(own, 24)
    pki[...] = jnp.transpose(own[...].astype(F32)).astype(BF)

    pl.semaphore_wait(barrier, NH + NC - 2)

    mine = block(me_h)

    def send_small(r, z):
        to = hpeer(r)
        remote(pki.at[heads(to), :], pkr.at[heads(me_h), :], 0, "head", to)
        return z

    lax.fori_loop(1, NH, send_small, 0)
    local(pki.at[heads(me_h), :], pkr.at[heads(me_h), :], 0)

    def send_maps(to):
        remote(bm, sm.at[0, mine, :], 1, "head", to)
        remote(cm, sm.at[1, mine, :], 1, "head", to)

    def send_maps_chip(r, z):
        send_maps(2 * lax.rem(chip + r, CHIPS) + core)
        return z

    lax.fori_loop(1, CHIPS, send_maps_chip, 0)
    send_maps(sibling)
    local(bm, sm.at[0, mine, :], 1)
    local(cm, sm.at[1, mine, :], 1)

    def send_wide(src, dst, s, h):
        def cols(k):
            return pl.ds(pl.multiple_of(k * W + h * HW, HW), HW)

        half = pl.ds(h * HW, HW)

        def one(r, z):
            to = hpeer(r)
            remote(src.at[:, cols(to)], dst.at[mine, half], s, "head", to)
            return z

        lax.fori_loop(1, NH, one, 0)
        local(src.at[:, cols(me_h)], dst.at[mine, half], s)

    send_wide(g, gb, 3, 0)
    send_wide(g, gb, 4, 1)
    send_wide(x, xb, 5, 0)
    send_wide(x, xb, 6, 1)

    arrived(pkr, 0)
    turned = jnp.transpose(pkr[...].astype(F32)).astype(BF)
    for k in range(NH):
        part = dot(turned, ones_where((row == k * GH + col) & (col < GH)))
        stc[k * TOK : (k + 1) * TOK, :] = part[0:TOK, :]
        cumc[k * TOK : (k + 1) * TOK, :] = part[TOK:, :]
    tots = []
    for c in range(CH):
        at = slice(c * Q, (c + 1) * Q)
        cum = dot(tri[...], cumc[at, :].astype(BF))
        cumc[at, :] = cum
        tots.append(cum[Q - 1 : Q, :])
    upto = [tots[0]]
    for c in range(1, CH):
        upto.append(upto[-1] + tots[c])
    beyond = [None] * CH
    beyond[CH - 1] = jnp.zeros_like(tots[0])
    for c in range(CH - 2, -1, -1):
        beyond[c] = beyond[c + 1] + tots[c + 1]
    for k in range(CH):
        prod[k : k + 1, 0:N] = tots[k]
        prod[CH + k : CH + k + 1, 0:N] = upto[k]
        prod[2 * CH + k : 2 * CH + k + 1, 0:N] = beyond[k]
        prod[3 * CH + k : 3 * CH + k + 1, 0:N] = jnp.zeros_like(tots[0])
    rows = jnp.exp(prod[:, 0:N])
    hi = rows.astype(BF)
    mid, low = halves(rows - hi.astype(F32))
    rowf[...] = dot(jnp.concatenate([hi, mid], axis=1), rep[...]) + dot(low, rep[0:N, :])
    for a in range(LG):
        for h in range(2):
            lanes = slice(h * HW + a * N, h * HW + (a + 1) * N)
            dec[a, h] = rowf[2 * CH - 1 : 2 * CH, lanes]

    def send_decay(r, z):
        k = cpeer(r)
        remote(dec.at[k // RG], decr.at[me_c], 7, "ctx", k)
        return z

    lax.fori_loop(1, NC, send_decay, 0)
    local(dec.at[me_c // RG], decr.at[me_c], 7)

    arrived(sm.at[:, pl.ds(0, 5 * TOK), :], 1)

    def pass_maps(r, z):
        at = block(2 * lax.rem(chip + r, CHIPS) + core)
        remote(sm.at[:, at, :], sm.at[:, at, :], 2, "head", sibling)
        return z

    lax.fori_loop(1, CHIPS, pass_maps, 0)

    def chunk(c):
        return pl.ds(pl.multiple_of(c * Q, Q), Q)

    def expand(a):
        return dot(jnp.concatenate(halves(a), axis=1), rep[...])

    for c in range(CH):
        at = slice(c * Q, (c + 1) * Q)
        cum = cumc[at, :]
        s = stc[at, :]
        f1[at, :] = expand(jnp.exp(cum))
        f2[at, :] = expand(s * jnp.exp(-cum))
        f1d[at, :] = expand(jnp.exp(cum + (upto[c] - tots[c])))
        f2d[at, :] = expand(s * jnp.exp(tots[c] - cum + beyond[c]))

    arrived(sm.at[:, pl.ds(0, 3 * TOK), :], 2)

    def transposed(a, out, c):
        t = jnp.transpose(a.astype(F32)).astype(BF)
        out[c, :, 0:Q] = t
        out[c, :, Q : 2 * Q] = t

    for c in range(CH):
        at = slice(c * Q, (c + 1) * Q)
        transposed(sm[0, at, :], bt2, c)
        transposed(sm[1, at, :], ct2, c)

    def stage(src, dst, h):
        for k in range(NC):
            a, b = k % RG * RB, h * HW + k // RG * N
            dst[h, k] = src[a : a + RB, b : b + N].astype(dst.dtype)

    def unstage(src, dst):
        for h in range(2):
            for k in range(NC):
                a, b = k % RG * RB, h * HW + k // RG * N
                dst[a : a + RB, b : b + N] = src[h, k].astype(dst.dtype)

    def spread(src, dst, s, h):
        def one(r, z):
            k = cpeer(r)
            remote(src.at[h, k], dst.at[h, me_c], s + h, "ctx", k)
            return z

        lax.fori_loop(1, NC, one, 0)
        local(src.at[h, me_c], dst.at[h, me_c], s + h)

    acc[...] = jnp.zeros_like(acc)
    for h in range(2):
        half = slice(h * HW, (h + 1) * HW)
        arrived(gb.at[:, pl.ds(h * HW, HW)], 3 + h)

        def step_g(r, z, half=half):
            c = CH - 1 - r
            at = chunk(c)
            ghi, glo = halves(gb[at, half].astype(F32) * f1[at, half])
            gx[c, 0:Q, half] = ghi
            end = acc[:, half]
            lg[c, :, half] = end
            end = end * rowf[pl.ds(c, 1), half]
            gx[c, Q : 2 * Q, half] = end.astype(BF)
            acc[:, half] = end + dot(ct2[c], jnp.concatenate([ghi, glo], axis=0))
            return z

        lax.fori_loop(0, CH, step_g, 0)
        stage(acc, gs, h)
        spread(gs, gr, 8, h)

    def step_u(c, z):
        at = chunk(c)
        b = sm[0, at, :]
        cb = jnp.where(above, dot(b, sm[1, at, :], NT), 0.0).astype(BF)
        v[at, :] = f2[at, :] * dot(jnp.concatenate([cb, b], axis=1), gx[c])
        return z

    lax.fori_loop(0, CH, step_u, 0)

    arrived(decr, 7)
    for h in range(2):
        arrived(gr.at[h], 8 + h)

        def back_g(r, carry, h=h):
            i = NC - 1 - r
            gbs[h, i] = carry.astype(BF)
            gf32[h, i] = carry
            return carry * decr[i, h] + gr[h, i].astype(F32)

        lax.fori_loop(0, NC, back_g, jnp.zeros((RB, N), F32))
        spread(gbs, gbr, 10, h)

    acc[...] = jnp.zeros_like(acc)
    for h in range(2):
        half = slice(h * HW, (h + 1) * HW)
        arrived(xb.at[:, pl.ds(h * HW, HW)], 5 + h)

        def step_x(c, z, half=half):
            at = chunk(c)
            xhi, xlo = halves(xb[at, half].astype(F32) * f2[at, half])
            xs[c, 0:Q, half] = xhi
            start = acc[:, half]
            ls[c, :, half] = start
            xs[c, Q : 2 * Q, half] = start.astype(BF)
            more = dot(bt2[c], jnp.concatenate([xhi, xlo], axis=0))
            acc[:, half] = (start + more) * rowf[pl.ds(c, 1), half]
            return z

        lax.fori_loop(0, CH, step_x, 0)
        ls[CH, :, half] = acc[:, half]
        stage(acc, ss, h)
        spread(ss, sr, 12, h)

    arrived(gbr.at[0], 10)
    arrived(gbr.at[1], 11)
    unstage(gbr, gin)

    def cols(k):
        return pl.ds(pl.multiple_of(k * W, W), W)

    def make_dx(p):
        at = chunk(p)
        now = v[at, :] + f2d[at, :] * dot(sm[0, at, :], gin[...])
        v[at, :] = now
        dxb[at, :] = (now + skip_row * gb[at, :].astype(F32)).astype(BF)

    def send_dx(to):
        remote(dxb.at[block(to), :], ox.at[:, cols(me_h)], 18, "head", to)

    def step_dx(r, z):
        p = lax.rem(chip + r, CHIPS)
        make_dx(p)
        send_dx(2 * p)
        send_dx(2 * p + 1)
        return z

    lax.fori_loop(1, CHIPS, step_dx, 0)
    make_dx(chip)
    send_dx(sibling)
    local(dxb.at[mine, :], ox.at[:, cols(me_h)], 18)

    for h in range(2):
        arrived(sr.at[h], 12 + h)

        def back_s(i, carry, h=h):
            sbs[h, i] = carry.astype(BF)
            pairs[h, i] = jnp.sum(carry * gf32[h, i], axis=0, keepdims=True)
            return carry * decr[i, h] + sr[h, i].astype(F32)

        lax.fori_loop(0, NC, back_s, jnp.zeros((RB, N), F32))
        spread(sbs, sbr, 14, h)
        spread(pairs, pairr, 16, h)

    def heads_sum(a):
        hi, lo = halves(a)
        return dot(hi, rep[0:N, :], NT) + dot(lo, rep[0:N, :], NT)

    def step_local(c, z):
        at = chunk(c)
        b, cc = sm[0, at, :], sm[1, at, :]
        gh, xh = gx[c, 0:Q, :], xs[c, 0:Q, :]
        xf, gf = xb[at, :].astype(F32), gb[at, :].astype(F32)
        cs[at, :] = heads_sum(xf * v[at, :])
        e = jnp.where(below, dot(gh, xh, NT), 0.0).astype(BF)
        et = jnp.where(above, dot(xh, gh, NT), 0.0).astype(BF)
        gk = (
            dot(et, cc)
            + dot(xh, gx[c, Q : 2 * Q, :], NT)
            + dot((xf * f2d[at, :]).astype(BF), gin[...], NT)
        )
        gq = dot(e, b) + dot(gh, xs[c, Q : 2 * Q, :], NT)
        for k in range(2):
            gbp[c, k] = gk[k * TOK : (k + 1) * TOK, :]
            gcp[c, k] = gq[k * TOK : (k + 1) * TOK, :]
        cb = jnp.where(below, dot(cc, b, NT), 0.0).astype(BF)
        y = f1[at, :] * dot(jnp.concatenate([cb, cc], axis=1), xs[c])
        rs[at, :] = heads_sum(gf * y)
        return z

    lax.fori_loop(0, CH, step_local, 0)

    def share(src, dst, s):
        remote(src.at[:, 1 - core], dst, s, "head", sibling)

    def share_far(src, dst, near, out, s, s2):
        arrived(dst, s)
        near[...] = src[:, pl.ds(core, 1)].reshape(CHIPS, TOK, N) + dst[...]

        def one(r, z):
            p = lax.rem(chip + r, CHIPS)
            remote(near.at[p], out.at[chip], s2, "head", 2 * p + core)
            return z

        lax.fori_loop(1, CHIPS, one, 0)
        local(near.at[chip], out.at[chip], s2)

    share(gbp, gbo, 19)

    arrived(sbr.at[0], 14)
    arrived(sbr.at[1], 15)
    unstage(sbr, sin)
    share_far(gbp, gbo, gbh, gbrv, 19, 20)

    def step_s(c, z):
        at = chunk(c)
        gf = gb[at, :].astype(F32)
        gd = gf * f1d[at, :]
        gq = dot(gd.astype(BF), sin[...], NT)
        for k in range(2):
            gcp[c, k] = gcp[c, k] + gq[k * TOK : (k + 1) * TOK, :]
        rs[at, :] = rs[at, :] + heads_sum(gd * dot(sm[1, at, :], sin[...]))
        return z

    lax.fori_loop(0, CH, step_s, 0)
    share(gcp, gco, 21)

    arrived(pairr.at[0], 16)
    arrived(pairr.at[1], 17)
    gi, si = gin[...].astype(F32), sin[...].astype(F32)
    exact = []
    for h in range(2):
        for a in range(LG):
            exact.append(jnp.sum(pairr[h, a * RG : (a + 1) * RG], axis=0))
    fix = rowf[2 * CH - 1 : 2 * CH, :] * (
        jnp.concatenate(exact, axis=1) - jnp.sum(gi * si, axis=0, keepdims=True)
    )
    prod[...] = jnp.zeros_like(prod)
    for c in range(CH):
        ge = lg[c] + rowf[2 * CH + c : 2 * CH + c + 1, :] * gi
        se = ls[c + 1] + rowf[CH + c : CH + c + 1, :] * si
        prod[c : c + 1, :] = jnp.sum(ge * se, axis=0, keepdims=True) + fix
    base = heads_sum(prod[...])
    lane = iota((Q, N), 1)
    upper = ones_where(above)
    packed = jnp.zeros((2 * TOK, N), F32)
    for c in range(CH):
        at = slice(c * Q, (c + 1) * Q)
        csum = cs[at, :]
        hi, lo = halves(rs[at, :] - csum)
        dq = base[c : c + 1, :] + dot(upper, hi) + dot(upper, lo)
        ds = jnp.where(lane < GH, csum / jnp.where(lane < GH, stc[at, :], 1.0), 0.0)
        for k in range(2):
            half = slice(k * TOK, (k + 1) * TOK)
            both = jnp.concatenate([ds[half, :], dq[half, :]], axis=0)
            turn = (2 * c + k) * GH
            packed = packed + (pltpu.roll(both, turn, 1) if turn else both)
    pko[...] = jnp.transpose(packed).astype(BF)

    def send_pk(r, z):
        to = hpeer(r)
        remote(pko.at[heads(to), :], pkv.at[heads(me_h), :], 23, "head", to)
        return z

    lax.fori_loop(1, NH, send_pk, 0)
    local(pko.at[heads(me_h), :], pkv.at[heads(me_h), :], 23)

    share_far(gcp, gco, gch, gcrv, 21, 22)

    arrived(gbrv, 20)
    ogb[...] = jnp.sum(gbrv[...], axis=0)
    arrived(pkv, 23)
    back = jnp.transpose(pkv[...].astype(F32)).astype(BF)
    ods[...] = back[0:TOK, :]
    odq[...] = back[TOK:, :]
    arrived(gcrv, 22)
    ogc[...] = jnp.sum(gcrv[...], axis=0)
    arrived(ox, 18)

    left(pkr.at[pl.ds(0, N - GH), :], 0)
    left(sm.at[:, pl.ds(0, 4 * TOK), :], 1)
    left(sm.at[:, pl.ds(0, 3 * TOK), :], 2)
    for h in range(2):
        left(gb.at[pl.ds(0, LEN - TOK), pl.ds(0, HW)], 3 + h)
        left(xb.at[pl.ds(0, LEN - TOK), pl.ds(0, HW)], 5 + h)
        left(gs.at[h, pl.ds(0, NC - 1)], 8 + h)
        left(gbs.at[h, pl.ds(0, NC - 1)], 10 + h)
        left(ss.at[h, pl.ds(0, NC - 1)], 12 + h)
        left(sbs.at[h, pl.ds(0, NC - 1)], 14 + h)
        left(pairs.at[h, pl.ds(0, NC - 1)], 16 + h)
    left(decr.at[pl.ds(0, NC - 1)], 7)
    left(dxb.at[pl.ds(0, LEN - TOK), :], 18)
    left(gbo, 19)
    left(gbh.at[pl.ds(0, CHIPS - 1)], 20)
    left(gco, 21)
    left(gch.at[pl.ds(0, CHIPS - 1)], 22)
    left(pkv.at[pl.ds(0, N - GH), :], 23)


def body(inputs, grad_out, steps, log_decay, input_map, output_map, skip_gain):
    hbm = pl.BlockSpec(memory_space=pl.ANY)
    vmem = pl.BlockSpec(memory_space=pltpu.VMEM)

    def vm(shape, kind):
        return pltpu.VMEM(shape, kind)

    grads = pl.pallas_call(
        kernel,
        out_shape=(
            jax.ShapeDtypeStruct((TOK, NH * W), BF),
            jax.ShapeDtypeStruct((TOK, N), BF),
            jax.ShapeDtypeStruct((TOK, N), BF),
            jax.ShapeDtypeStruct((TOK, N), F32),
            jax.ShapeDtypeStruct((TOK, N), F32),
        ),
        in_specs=[hbm] * 6 + [vmem],
        out_specs=(hbm, vmem, vmem, vmem, vmem),
        scratch_shapes=[
            vm((LEN, W), BF),
            vm((LEN, W), BF),
            vm((2, LEN, N), BF),
            vm((2 * TOK, N), BF),
            vm((N, 2 * TOK), BF),
            vm((N, 2 * TOK), BF),
            vm((2 * N, W), BF),
            vm((LEN, W), F32),
            vm((LEN, W), F32),
            vm((LEN, W), F32),
            vm((LEN, W), F32),
            vm((4 * CH, W), F32),
            vm((Q, Q), BF),
            vm((LEN, N), F32),
            vm((LEN, N), F32),
            vm((CH, N, 2 * Q), BF),
            vm((CH, N, 2 * Q), BF),
            vm((CH, 2 * Q, W), BF),
            vm((CH, 2 * Q, W), BF),
            vm((CH, N, W), F32),
            vm((CH + 1, N, W), F32),
            vm((N, W), F32),
            vm((LEN, W), F32),
            vm((LEN, W), BF),
            vm((N, W), BF),
            vm((N, W), BF),
            vm((LG, 2, 1, N), F32),
            vm((NC, 2, 1, N), F32),
            vm((2, NC, RB, N), BF),
            vm((2, NC, RB, N), BF),
            vm((2, NC, RB, N), BF),
            vm((2, NC, RB, N), BF),
            vm((2, NC, RB, N), F32),
            vm((2, NC, RB, N), BF),
            vm((2, NC, RB, N), BF),
            vm((2, NC, RB, N), BF),
            vm((2, NC, RB, N), BF),
            vm((2, NC, 1, N), F32),
            vm((2, NC, 1, N), F32),
            vm((LEN, N), F32),
            vm((LEN, N), F32),
            vm((4 * CH, W), F32),
            vm((CHIPS, 2, TOK, N), F32),
            vm((CHIPS, 2, TOK, N), F32),
            vm((CHIPS, TOK, N), F32),
            vm((CHIPS, TOK, N), F32),
            vm((CHIPS, TOK, N), F32),
            vm((CHIPS, TOK, N), F32),
            vm((CHIPS, TOK, N), F32),
            vm((CHIPS, TOK, N), F32),
            vm((N, 2 * TOK), BF),
            vm((N, 2 * TOK), BF),
            pltpu.SemaphoreType.DMA((24,)),
            pltpu.SemaphoreType.DMA((25,)),
        ],
        compiler_params=pltpu.CompilerParams(
            collective_id=0, has_side_effects=True, vmem_limit_bytes=56 * 1024 * 1024
        ),
        cost_estimate=pl.CostEstimate(
            flops=3 * 10**9, bytes_accessed=8 * 2**20, transcendentals=2**20
        ),
        name="block_backward",
    )(inputs, grad_out, steps, log_decay, input_map, output_map, skip_gain.reshape(1, GH))
    return grads


def solution(mesh):
    spread = P(("ctx", "head"), None)
    return jax.shard_map(
        body,
        mesh=mesh,
        in_specs=(spread,) * 6 + (P("head"),),
        out_specs=(spread,) * 5,
        check_vma=False,
    )
```

time: 83.2 us -> 70 us (0.84)
  Pallas kernels: 77.4 us -> 64.2 us
    pallas_call x1, Pallas kernels: 77.4 us -> 64.2 us  [body(): pl.pallas_call(kernel, out_shape=(jax.ShapeDtypeStruct((TOK, NH * W), BF)...]
where the time goes in v1:
time: 70 us; the launch traced here: 69.7 us
  Pallas kernels  64.2 us (92%)
  local copies, waits for them, and re-layouts  4.88 us (7%)
    pallas_call x1, Pallas kernels, body(): pl.pallas_call(kernel, out_shape=(jax.ShapeDtypeStruct((TOK, NH * W), BF)...  64.2 us
    unnamed x13, local copies, waits for them, and re-layouts  4.88 us

profile of v1, /device:TPU:1, one launch (start us, length us, event | category | flops | bytes accessed | tf_op | source)
XLA Modules:
  0.0 69.7 jit_solution(7859132783367857111)
XLA Ops:
  0.6 64.2 %block_backward.1 = (bf16[64,8192]{1,0:T(8,128)(2,1)}, bf16[64,128]{1,0:T(8,128)(2,1)}, bf16[64,128]{1,0:T(8,128)(2,1)}, f32[64,128]{1,0:T(8,128)}, f32[64,128]{1,0:T(8,128)}) custom-call(bf16[64,8192]{1,0:T(8,128)(2,1)} %x.1, bf16[64,8192]{1,0:T(8,128)(2,1)} %g.1, bf16[64,128]{1,0:T(8,128)(2,1)} %st.1, bf16[64,128]{1,0:T(8,128)(2,1)} %ld.1, ...), custom_call_target="tpu_custom_call" | custom-call | flops 3000000000 | bytes 8388608 | tf_op jit(solution)/shard_map/block_backward/pallas_call | solution.py:504
  64.8 0.0 copy-start.3
  64.8 0.0 copy-start.2
  64.9 2.3 %copy.17 = bf16[64,8192]{1,0:T(8,128)(2,1)} copy(bf16[64,8192]{1,0:T(8,128)(2,1)} %get-tuple-element.10) | data formatting | bytes 2097152
  67.1 0.0 copy-done.3
  67.1 0.0 copy-start.1
  67.1 0.6 copy.18
  67.7 0.0 copy-done.2
  67.7 0.6 copy.19
  68.3 0.0 copy-done.1
  68.3 0.0 copy-start
  68.4 0.6 copy.20
  69.0 0.2 copy-done
  69.1 0.6 copy.21
Async XLA Ops:
  64.8 2.3 %copy-start.3 = (bf16[64,128]{1,0:T(8,128)(2,1)S(1)}, bf16[64,128]{1,0:T(8,128)(2,1)}, u32[]{:S(2)}) copy-start(bf16[64,128]{1,0:T(8,128)(2,1)} %get-tuple-element.11) | copy-start | bytes 49156
  64.8 2.9 %copy-start.2 = (bf16[64,128]{1,0:T(8,128)(2,1)S(1)}, bf16[64,128]{1,0:T(8,128)(2,1)}, u32[]{:S(2)}) copy-start(bf16[64,128]{1,0:T(8,128)(2,1)} %get-tuple-element.12) | copy-start | bytes 49156
  67.1 1.2 %copy-start.1 = (f32[64,128]{1,0:T(8,128)S(1)}, f32[64,128]{1,0:T(8,128)}, u32[]{:S(2)}) copy-start(f32[64,128]{1,0:T(8,128)} %get-tuple-element.13) | copy-start | bytes 98308
  68.3 0.8 %copy-start = (f32[64,128]{1,0:T(8,128)S(1)}, f32[64,128]{1,0:T(8,128)}, u32[]{:S(2)}) copy-start(f32[64,128]{1,0:T(8,128)} %get-tuple-element.14) | copy-start | bytes 98308

commit v2 on v1

--- a/solution.py
+++ b/solution.py
@@ -46,10 +46,10 @@
 
 
 def kernel(
-    x, g, st, ld, bm, cm, skip, ox, ods, odq, ogb, ogc,
+    x, g, st, ld, bm, cm, skip, ox, pkv, gbrv, gcrv,
     gb, xb, sm, own, pki, pkr, rep, f1, f2, f1d, f2d, rowf, tri, stc, cumc, ct2, bt2, gx, xs,
     lg, ls, acc, v, dxb, gin, sin, dec, decr, gs, gr, gbs, gbr, gf32, ss, sr, sbs, sbr, pairs, pairr,
-    cs, rs, prod, gbp, gcp, gbo, gco, gbh, gch, gbrv, gcrv, pko, pkv, send, recv,
+    cs, rs, prod, gbp, gcp, gbo, gbh, gcb, pko, send, recv,
 ):
     me_c = lax.axis_index("ctx")
     me_h = lax.axis_index("head")
@@ -240,11 +240,10 @@
             a, b = k % RG * RB, h * HW + k // RG * N
             dst[h, k] = src[a : a + RB, b : b + N].astype(dst.dtype)
 
-    def unstage(src, dst):
-        for h in range(2):
-            for k in range(NC):
-                a, b = k % RG * RB, h * HW + k // RG * N
-                dst[a : a + RB, b : b + N] = src[h, k].astype(dst.dtype)
+    def unstage(src, dst, h):
+        for k in range(NC):
+            a, b = k % RG * RB, h * HW + k // RG * N
+            dst[a : a + RB, b : b + N] = src[h, k]
 
     def spread(src, dst, s, h):
         def one(r, z):
@@ -255,12 +254,39 @@
         lax.fori_loop(1, NC, one, 0)
         local(src.at[h, me_c], dst.at[h, me_c], s + h)
 
-    acc[...] = jnp.zeros_like(acc)
-    for h in range(2):
-        half = slice(h * HW, (h + 1) * HW)
+    def half_of(h):
+        return slice(h * HW, (h + 1) * HW)
+
+    def local_u(h):
+        half = half_of(h)
+
+        def step_u(c, z):
+            at = chunk(c)
+            b = sm[0, at, :]
+            cb = jnp.where(above, dot(b, sm[1, at, :], NT), 0.0).astype(BF)
+            v[at, half] = f2[at, half] * dot(jnp.concatenate([cb, b], axis=1), gx[c, :, half])
+            return z
+
+        lax.fori_loop(0, CH, step_u, 0)
+
+    def owners_g(h):
+        arrived(gr.at[h], 8 + h)
+
+        def back_g(r, carry):
+            i = NC - 1 - r
+            gbs[h, i] = carry.astype(BF)
+            gf32[h, i] = carry
+            return carry * decr[i, h] + gr[h, i].astype(F32)
+
+        lax.fori_loop(0, NC, back_g, jnp.zeros((RB, N), F32))
+        spread(gbs, gbr, 10, h)
+
+    def local_g(h):
+        half = half_of(h)
         arrived(gb.at[:, pl.ds(h * HW, HW)], 3 + h)
-
-        def step_g(r, z, half=half):
+        acc[:, half] = jnp.zeros((N, HW), F32)
+
+        def step_g(r, z):
             c = CH - 1 - r
             at = chunk(c)
             ghi, glo = halves(gb[at, half].astype(F32) * f1[at, half])
@@ -276,34 +302,12 @@
         stage(acc, gs, h)
         spread(gs, gr, 8, h)
 
-    def step_u(c, z):
-        at = chunk(c)
-        b = sm[0, at, :]
-        cb = jnp.where(above, dot(b, sm[1, at, :], NT), 0.0).astype(BF)
-        v[at, :] = f2[at, :] * dot(jnp.concatenate([cb, b], axis=1), gx[c])
-        return z
-
-    lax.fori_loop(0, CH, step_u, 0)
-
-    arrived(decr, 7)
-    for h in range(2):
-        arrived(gr.at[h], 8 + h)
-
-        def back_g(r, carry, h=h):
-            i = NC - 1 - r
-            gbs[h, i] = carry.astype(BF)
-            gf32[h, i] = carry
-            return carry * decr[i, h] + gr[h, i].astype(F32)
-
-        lax.fori_loop(0, NC, back_g, jnp.zeros((RB, N), F32))
-        spread(gbs, gbr, 10, h)
-
-    acc[...] = jnp.zeros_like(acc)
-    for h in range(2):
-        half = slice(h * HW, (h + 1) * HW)
+    def local_x(h):
+        half = half_of(h)
         arrived(xb.at[:, pl.ds(h * HW, HW)], 5 + h)
-
-        def step_x(c, z, half=half):
+        acc[:, half] = jnp.zeros((N, HW), F32)
+
+        def step_x(c, z):
             at = chunk(c)
             xhi, xlo = halves(xb[at, half].astype(F32) * f2[at, half])
             xs[c, 0:Q, half] = xhi
@@ -319,49 +323,69 @@
         stage(acc, ss, h)
         spread(ss, sr, 12, h)
 
-    arrived(gbr.at[0], 10)
-    arrived(gbr.at[1], 11)
-    unstage(gbr, gin)
-
-    def cols(k):
-        return pl.ds(pl.multiple_of(k * W, W), W)
-
-    def make_dx(p):
-        at = chunk(p)
-        now = v[at, :] + f2d[at, :] * dot(sm[0, at, :], gin[...])
-        v[at, :] = now
-        dxb[at, :] = (now + skip_row * gb[at, :].astype(F32)).astype(BF)
-
-    def send_dx(to):
-        remote(dxb.at[block(to), :], ox.at[:, cols(me_h)], 18, "head", to)
-
-    def step_dx(r, z):
-        p = lax.rem(chip + r, CHIPS)
-        make_dx(p)
-        send_dx(2 * p)
-        send_dx(2 * p + 1)
-        return z
-
-    lax.fori_loop(1, CHIPS, step_dx, 0)
-    make_dx(chip)
-    send_dx(sibling)
-    local(dxb.at[mine, :], ox.at[:, cols(me_h)], 18)
-
-    for h in range(2):
+    def channels(h):
+        half = half_of(h)
+        arrived(gbr.at[h], 10 + h)
+        unstage(gbr, gin, h)
+        there = pl.ds(pl.multiple_of(me_h * W + h * HW, HW), HW)
+
+        def make_dx(p):
+            at = chunk(p)
+            now = v[at, half] + f2d[at, half] * dot(sm[0, at, :], gin[:, half])
+            v[at, half] = now
+            dxb[at, half] = (now + skip_row[:, half] * gb[at, half].astype(F32)).astype(BF)
+
+        def send_dx(to):
+            remote(dxb.at[block(to), pl.ds(h * HW, HW)], ox.at[:, there], 18, "head", to)
+
+        def step_dx(r, z):
+            p = lax.rem(chip + r, CHIPS)
+            make_dx(p)
+            send_dx(2 * p)
+            send_dx(2 * p + 1)
+            return z
+
+        lax.fori_loop(1, CHIPS, step_dx, 0)
+        make_dx(chip)
+        send_dx(sibling)
+        local(dxb.at[mine, pl.ds(h * HW, HW)], ox.at[:, there], 18)
+
+    def owners_s(h):
         arrived(sr.at[h], 12 + h)
 
-        def back_s(i, carry, h=h):
+        def back_s(i, carry):
             sbs[h, i] = carry.astype(BF)
-            pairs[h, i] = jnp.sum(carry * gf32[h, i], axis=0, keepdims=True)
+            pairs[i, h] = jnp.sum(carry * gf32[h, i], axis=0, keepdims=True)
             return carry * decr[i, h] + sr[h, i].astype(F32)
 
         lax.fori_loop(0, NC, back_s, jnp.zeros((RB, N), F32))
         spread(sbs, sbr, 14, h)
-        spread(pairs, pairr, 16, h)
-
-    def heads_sum(a):
+
+    local_g(0)
+    local_u(0)
+    local_g(1)
+    arrived(decr, 7)
+    owners_g(0)
+    local_u(1)
+    owners_g(1)
+    local_x(0)
+    channels(0)
+    local_x(1)
+    channels(1)
+    owners_s(0)
+    owners_s(1)
+
+    def send_pairs(r, z):
+        k = cpeer(r)
+        remote(pairs.at[k], pairr.at[me_c], 16, "ctx", k)
+        return z
+
+    lax.fori_loop(1, NC, send_pairs, 0)
+    local(pairs.at[me_c], pairr.at[me_c], 16)
+
+    def heads_sum(a, half=slice(0, W)):
         hi, lo = halves(a)
-        return dot(hi, rep[0:N, :], NT) + dot(lo, rep[0:N, :], NT)
+        return dot(hi, rep[0:N, half], NT) + dot(lo, rep[0:N, half], NT)
 
     def step_local(c, z):
         at = chunk(c)
@@ -386,49 +410,56 @@
         return z
 
     lax.fori_loop(0, CH, step_local, 0)
-
-    def share(src, dst, s):
-        remote(src.at[:, 1 - core], dst, s, "head", sibling)
-
-    def share_far(src, dst, near, out, s, s2):
-        arrived(dst, s)
-        near[...] = src[:, pl.ds(core, 1)].reshape(CHIPS, TOK, N) + dst[...]
-
-        def one(r, z):
-            p = lax.rem(chip + r, CHIPS)
-            remote(near.at[p], out.at[chip], s2, "head", 2 * p + core)
+    remote(gbp.at[:, 1 - core], gbo, 19, "head", sibling)
+
+    def use_s(h):
+        half = half_of(h)
+        arrived(sbr.at[h], 14 + h)
+        unstage(sbr, sin, h)
+
+        def step_s(c, z):
+            at = chunk(c)
+            gd = gb[at, half].astype(F32) * f1d[at, half]
+            gq = dot(gd.astype(BF), sin[:, half], NT)
+            for k in range(2):
+                now = gcp[c, k] + gq[k * TOK : (k + 1) * TOK, :]
+                if h == 0:
+                    gcp[c, k] = now
+                else:
+                    gcb[c, k] = now.astype(BF)
+            rs[at, :] = rs[at, :] + heads_sum(gd * dot(sm[1, at, :], sin[:, half]), half)
             return z
 
-        lax.fori_loop(1, CHIPS, one, 0)
-        local(near.at[chip], out.at[chip], s2)
-
-    share(gbp, gbo, 19)
-
-    arrived(sbr.at[0], 14)
-    arrived(sbr.at[1], 15)
-    unstage(sbr, sin)
-    share_far(gbp, gbo, gbh, gbrv, 19, 20)
-
-    def step_s(c, z):
-        at = chunk(c)
-        gf = gb[at, :].astype(F32)
-        gd = gf * f1d[at, :]
-        gq = dot(gd.astype(BF), sin[...], NT)
-        for k in range(2):
-            gcp[c, k] = gcp[c, k] + gq[k * TOK : (k + 1) * TOK, :]
-        rs[at, :] = rs[at, :] + heads_sum(gd * dot(sm[1, at, :], sin[...]))
-        return z
-
-    lax.fori_loop(0, CH, step_s, 0)
-    share(gcp, gco, 21)
-
-    arrived(pairr.at[0], 16)
-    arrived(pairr.at[1], 17)
+        lax.fori_loop(0, CH, step_s, 0)
+
+    use_s(0)
+    arrived(gbo, 19)
+    gbh[...] = gbp[:, pl.ds(core, 1)].reshape(CHIPS, TOK, N) + gbo[...]
+
+    def send_gb(r, z):
+        p = lax.rem(chip + r, CHIPS)
+        remote(gbh.at[p], gbrv.at[chip], 20, "head", 2 * p + core)
+        return z
+
+    lax.fori_loop(1, CHIPS, send_gb, 0)
+    local(gbh.at[chip], gbrv.at[chip], 20)
+
+    use_s(1)
+
+    def send_gc(r, z):
+        to = hpeer(r)
+        remote(gcb.at[to // 2, lax.rem(to, 2)], gcrv.at[me_h], 21, "head", to)
+        return z
+
+    lax.fori_loop(1, NH, send_gc, 0)
+    local(gcb.at[chip, core], gcrv.at[me_h], 21)
+
+    arrived(pairr, 16)
     gi, si = gin[...].astype(F32), sin[...].astype(F32)
     exact = []
     for h in range(2):
         for a in range(LG):
-            exact.append(jnp.sum(pairr[h, a * RG : (a + 1) * RG], axis=0))
+            exact.append(jnp.sum(pairr[a * RG : (a + 1) * RG, h], axis=0))
     fix = rowf[2 * CH - 1 : 2 * CH, :] * (
         jnp.concatenate(exact, axis=1) - jnp.sum(gi * si, axis=0, keepdims=True)
     )
@@ -462,16 +493,9 @@
     lax.fori_loop(1, NH, send_pk, 0)
     local(pko.at[heads(me_h), :], pkv.at[heads(me_h), :], 23)
 
-    share_far(gcp, gco, gch, gcrv, 21, 22)
-
     arrived(gbrv, 20)
-    ogb[...] = jnp.sum(gbrv[...], axis=0)
     arrived(pkv, 23)
-    back = jnp.transpose(pkv[...].astype(F32)).astype(BF)
-    ods[...] = back[0:TOK, :]
-    odq[...] = back[TOK:, :]
-    arrived(gcrv, 22)
-    ogc[...] = jnp.sum(gcrv[...], axis=0)
+    arrived(gcrv, 21)
     arrived(ox, 18)
 
     left(pkr.at[pl.ds(0, N - GH), :], 0)
@@ -484,14 +508,24 @@
         left(gbs.at[h, pl.ds(0, NC - 1)], 10 + h)
         left(ss.at[h, pl.ds(0, NC - 1)], 12 + h)
         left(sbs.at[h, pl.ds(0, NC - 1)], 14 + h)
-        left(pairs.at[h, pl.ds(0, NC - 1)], 16 + h)
     left(decr.at[pl.ds(0, NC - 1)], 7)
+    left(pairr.at[pl.ds(0, NC - 1)], 16)
     left(dxb.at[pl.ds(0, LEN - TOK), :], 18)
     left(gbo, 19)
     left(gbh.at[pl.ds(0, CHIPS - 1)], 20)
-    left(gco, 21)
-    left(gch.at[pl.ds(0, CHIPS - 1)], 22)
+    left(gcrv.at[pl.ds(0, NH - 1)], 21)
     left(pkv.at[pl.ds(0, N - GH), :], 23)
+
+
+def finish(ox, pkv, gbrv, gcrv, odx, ods, odq, ogb, ogc, sem):
+    move = pltpu.make_async_copy(ox, odx, sem)
+    move.start()
+    back = jnp.transpose(pkv[...].astype(F32)).astype(BF)
+    ods[...] = back[0:TOK, :]
+    odq[...] = back[TOK:, :]
+    ogb[...] = jnp.sum(gbrv[...], axis=0)
+    ogc[...] = jnp.sum(gcrv[...].astype(F32), axis=0)
+    move.wait()
 
 
 def body(inputs, grad_out, steps, log_decay, input_map, output_map, skip_gain):
@@ -501,17 +535,16 @@
     def vm(shape, kind):
         return pltpu.VMEM(shape, kind)
 
-    grads = pl.pallas_call(
+    parts = pl.pallas_call(
         kernel,
         out_shape=(
             jax.ShapeDtypeStruct((TOK, NH * W), BF),
-            jax.ShapeDtypeStruct((TOK, N), BF),
-            jax.ShapeDtypeStruct((TOK, N), BF),
-            jax.ShapeDtypeStruct((TOK, N), F32),
-            jax.ShapeDtypeStruct((TOK, N), F32),
+            jax.ShapeDtypeStruct((N, 2 * TOK), BF),
+            jax.ShapeDtypeStruct((CHIPS, TOK, N), F32),
+            jax.ShapeDtypeStruct((NH, TOK, N), BF),
         ),
         in_specs=[hbm] * 6 + [vmem],
-        out_specs=(hbm, vmem, vmem, vmem, vmem),
+        out_specs=(hbm,) * 4,
         scratch_shapes=[
             vm((LEN, W), BF),
             vm((LEN, W), BF),
@@ -550,8 +583,8 @@
             vm((2, NC, RB, N), BF),
             vm((2, NC, RB, N), BF),
             vm((2, NC, RB, N), BF),
-            vm((2, NC, 1, N), F32),
-            vm((2, NC, 1, N), F32),
+            vm((NC, 2, 1, N), F32),
+            vm((NC, 2, 1, N), F32),
             vm((LEN, N), F32),
             vm((LEN, N), F32),
             vm((4 * CH, W), F32),
@@ -559,11 +592,7 @@
             vm((CHIPS, 2, TOK, N), F32),
             vm((CHIPS, TOK, N), F32),
             vm((CHIPS, TOK, N), F32),
-            vm((CHIPS, TOK, N), F32),
-            vm((CHIPS, TOK, N), F32),
-            vm((CHIPS, TOK, N), F32),
-            vm((CHIPS, TOK, N), F32),
-            vm((N, 2 * TOK), BF),
+            vm((CHIPS, 2, TOK, N), BF),
             vm((N, 2 * TOK), BF),
             pltpu.SemaphoreType.DMA((24,)),
             pltpu.SemaphoreType.DMA((25,)),
@@ -576,7 +605,21 @@
         ),
         name="block_backward",
     )(inputs, grad_out, steps, log_decay, input_map, output_map, skip_gain.reshape(1, GH))
-    return grads
+    return pl.pallas_call(
+        finish,
+        out_shape=(
+            jax.ShapeDtypeStruct((TOK, NH * W), BF),
+            jax.ShapeDtypeStruct((TOK, N), BF),
+            jax.ShapeDtypeStruct((TOK, N), BF),
+            jax.ShapeDtypeStruct((TOK, N), F32),
+            jax.ShapeDtypeStruct((TOK, N), F32),
+        ),
+        in_specs=[hbm, vmem, vmem, vmem],
+        out_specs=(hbm, vmem, vmem, vmem, vmem),
+        scratch_shapes=[pltpu.SemaphoreType.DMA],
+        cost_estimate=pl.CostEstimate(flops=2**20, bytes_accessed=3 * 2**20, transcendentals=0),
+        name="finish",
+    )(*parts)
 
 
 def solution(mesh):

time: 70 us -> 98 us (1.40)
  Pallas kernels: 64.2 us -> 97.1 us
  local copies, waits for them, and re-layouts: 4.88 us -> 0 us
    pallas_call x0 -> x1, Pallas kernels: none -> 34.5 us  [body(): pl.pallas_call(finish, out_shape=(jax.ShapeDtypeStruct((TOK, NH * W), BF)...]
    unnamed x13 -> x0, local copies, waits for them, and re-layouts: 4.88 us -> none
    pallas_call x1, Pallas kernels: 64.2 us -> 62.6 us  [body(): pl.pallas_call(kernel, out_shape=(jax.ShapeDtypeStruct((TOK, NH * W), BF)...]
where the time goes in v2:
time: 98 us; the launch traced here: 97.8 us
  Pallas kernels  97.1 us (99%)
    pallas_call x1, Pallas kernels, body(): pl.pallas_call(kernel, out_shape=(jax.ShapeDtypeStruct((TOK, NH * W), BF)...  62.6 us
    pallas_call x1, Pallas kernels, body(): pl.pallas_call(finish, out_shape=(jax.ShapeDtypeStruct((TOK, NH * W), BF)...  34.5 us

profile of v2, /device:TPU:1, one launch (start us, length us, event | category | flops | bytes accessed | tf_op | source)
XLA Modules:
  0.0 97.8 jit_solution(8116772441997311927)
XLA Ops:
  0.6 62.6 %block_backward.1 = (bf16[64,8192]{1,0:T(8,128)(2,1)}, bf16[128,128]{1,0:T(8,128)(2,1)}, f32[4,64,128]{2,1,0:T(8,128)}, bf16[8,64,128]{2,1,0:T(8,128)(2,1)}) custom-call(bf16[64,8192]{1,0:T(8,128)(2,1)} %x.1, bf16[64,8192]{1,0:T(8,128)(2,1)} %g.1, bf16[64,128]{1,0:T(8,128)(2,1)} %st.1, bf16[64,128]{1,0:T(8,128)(2,1)} %ld.1, bf16[64,128]{1,0:T(8,128)(2,1)} %bm.1, ...), custom_call_target="tpu_custom_call" | custom-call | flops 3000000000 | bytes 8388608 | tf_op jit(solution)/shard_map/block_backward/pallas_call | solution.py:538
  63.3 34.5 %finish.1 = (bf16[64,8192]{1,0:T(8,128)(2,1)}, bf16[64,128]{1,0:T(8,128)(2,1)}, bf16[64,128]{1,0:T(8,128)(2,1)}, f32[64,128]{1,0:T(8,128)}, f32[64,128]{1,0:T(8,128)}) custom-call(bf16[64,8192]{1,0:T(8,128)(2,1)} %get-tuple-element.9.ox, bf16[128,128]{1,0:T(8,128)(2,1)} %get-tuple-element.10.pkv, f32[4,64,128]{2,1,0:T(8,128)} %get-tuple-element.11.gbrv, ...), custom_call_target="tpu_custom_call" | custom-call | flops 1048576 | bytes 3145728 | tf_op jit(solution)/shard_map/finish/pallas_call | solution.py:608

commit v3 on v2

--- a/solution.py
+++ b/solution.py
@@ -538,13 +538,13 @@
     parts = pl.pallas_call(
         kernel,
         out_shape=(
-            jax.ShapeDtypeStruct((TOK, NH * W), BF),
-            jax.ShapeDtypeStruct((N, 2 * TOK), BF),
-            jax.ShapeDtypeStruct((CHIPS, TOK, N), F32),
-            jax.ShapeDtypeStruct((NH, TOK, N), BF),
+            vm((TOK, NH * W), BF),
+            vm((N, 2 * TOK), BF),
+            vm((CHIPS, TOK, N), F32),
+            vm((NH, TOK, N), BF),
         ),
         in_specs=[hbm] * 6 + [vmem],
-        out_specs=(hbm,) * 4,
+        out_specs=(vmem,) * 4,
         scratch_shapes=[
             vm((LEN, W), BF),
             vm((LEN, W), BF),
@@ -605,6 +605,7 @@
         ),
         name="block_backward",
     )(inputs, grad_out, steps, log_decay, input_map, output_map, skip_gain.reshape(1, GH))
+    parts = [pltpu.with_memory_space_constraint(part, pltpu.VMEM) for part in parts]
     return pl.pallas_call(
         finish,
         out_shape=(
@@ -614,7 +615,7 @@
             jax.ShapeDtypeStruct((TOK, N), F32),
             jax.ShapeDtypeStruct((TOK, N), F32),
         ),
-        in_specs=[hbm, vmem, vmem, vmem],
+        in_specs=[vmem] * 4,
         out_specs=(hbm, vmem, vmem, vmem, vmem),
         scratch_shapes=[pltpu.SemaphoreType.DMA],
         cost_estimate=pl.CostEstimate(flops=2**20, bytes_accessed=3 * 2**20, transcendentals=0),

time: 98 us -> 65.1 us (0.66)
  Pallas kernels: 97.1 us -> 64.2 us
    pallas_call x1, Pallas kernels: 34.5 us -> 1.62 us  [body(): pl.pallas_call(finish, out_shape=(jax.ShapeDtypeStruct((TOK, NH * W), BF)...]
where the time goes in v3:
time: 65.1 us; the launch traced here: 64.8 us
  Pallas kernels  64.2 us (99%)
    pallas_call x1, Pallas kernels, body(): pl.pallas_call(kernel, out_shape=(vm((TOK, NH * W), BF), vm((N, 2 * TOK),...  62.6 us
    pallas_call x1, Pallas kernels, body(): pl.pallas_call(finish, out_shape=(jax.ShapeDtypeStruct((TOK, NH * W), BF)...  1.62 us

profile of v3, /device:TPU:1, one launch (start us, length us, event | category | flops | bytes accessed | tf_op | source)
XLA Modules:
  0.0 64.8 jit_solution(7474341579197062376)
XLA Ops:
  0.6 62.6 %block_backward.1 = (bf16[64,8192]{1,0:T(8,128)(2,1)S(1)}, bf16[128,128]{1,0:T(8,128)(2,1)S(1)}, f32[4,64,128]{2,1,0:T(8,128)S(1)}, bf16[8,64,128]{2,1,0:T(8,128)(2,1)S(1)}) custom-call(bf16[64,8192]{1,0:T(8,128)(2,1)} %x.1, bf16[64,8192]{1,0:T(8,128)(2,1)} %g.1, bf16[64,128]{1,0:T(8,128)(2,1)} %st.1, bf16[64,128]{1,0:T(8,128)(2,1)} %ld.1, ...), custom_call_target="tpu_custom_call" | custom-call | flops 3000000000 | bytes 8388608 | tf_op jit(solution)/shard_map/block_backward/pallas_call | solution.py:538
  63.2 1.6 %finish.1 = (bf16[64,8192]{1,0:T(8,128)(2,1)}, bf16[64,128]{1,0:T(8,128)(2,1)}, bf16[64,128]{1,0:T(8,128)(2,1)}, f32[64,128]{1,0:T(8,128)}, f32[64,128]{1,0:T(8,128)}) custom-call(bf16[64,8192]{1,0:T(8,128)(2,1)S(1)} %get-tuple-element.9.ox, bf16[128,128]{1,0:T(8,128)(2,1)S(1)} %get-tuple-element.10.pkv, f32[4,64,128]{2,1,0:T(8,128)S(1)} %get-tuple-element.11.gbrv, ...), custom_call_target="tpu_custom_call" | custom-call | flops 1048576 | bytes 3145728 | tf_op jit(solution)/shard_map/finish/pallas_call | solution.py:609

commit v4 on v3

--- a/solution.py
+++ b/solution.py
@@ -23,6 +23,7 @@
 RG = N // RB
 LG = HW // N
 CHIPS = NH // 2
+EARLY = 1
 
 NN = ((1,), (0,))
 NT = ((1,), (1,))
@@ -361,28 +362,6 @@
         lax.fori_loop(0, NC, back_s, jnp.zeros((RB, N), F32))
         spread(sbs, sbr, 14, h)
 
-    local_g(0)
-    local_u(0)
-    local_g(1)
-    arrived(decr, 7)
-    owners_g(0)
-    local_u(1)
-    owners_g(1)
-    local_x(0)
-    channels(0)
-    local_x(1)
-    channels(1)
-    owners_s(0)
-    owners_s(1)
-
-    def send_pairs(r, z):
-        k = cpeer(r)
-        remote(pairs.at[k], pairr.at[me_c], 16, "ctx", k)
-        return z
-
-    lax.fori_loop(1, NC, send_pairs, 0)
-    local(pairs.at[me_c], pairr.at[me_c], 16)
-
     def heads_sum(a, half=slice(0, W)):
         hi, lo = halves(a)
         return dot(hi, rep[0:N, half], NT) + dot(lo, rep[0:N, half], NT)
@@ -409,7 +388,30 @@
         rs[at, :] = heads_sum(gf * y)
         return z
 
-    lax.fori_loop(0, CH, step_local, 0)
+    local_g(0)
+    local_u(0)
+    local_g(1)
+    arrived(decr, 7)
+    owners_g(0)
+    local_u(1)
+    owners_g(1)
+    local_x(0)
+    channels(0)
+    local_x(1)
+    channels(1)
+    lax.fori_loop(0, EARLY, step_local, 0)
+    owners_s(0)
+    owners_s(1)
+
+    def send_pairs(r, z):
+        k = cpeer(r)
+        remote(pairs.at[k], pairr.at[me_c], 16, "ctx", k)
+        return z
+
+    lax.fori_loop(1, NC, send_pairs, 0)
+    local(pairs.at[me_c], pairr.at[me_c], 16)
+
+    lax.fori_loop(EARLY, CH, step_local, 0)
     remote(gbp.at[:, 1 - core], gbo, 19, "head", sibling)
 
     def use_s(h):
@@ -417,7 +419,7 @@
         arrived(sbr.at[h], 14 + h)
         unstage(sbr, sin, h)
 
-        def step_s(c, z):
+        def use_chunk(c):
             at = chunk(c)
             gd = gb[at, half].astype(F32) * f1d[at, half]
             gq = dot(gd.astype(BF), sin[:, half], NT)
@@ -428,11 +430,36 @@
                 else:
                     gcb[c, k] = now.astype(BF)
             rs[at, :] = rs[at, :] + heads_sum(gd * dot(sm[1, at, :], sin[:, half]), half)
+
+        def send_gc(c, k, to):
+            remote(gcb.at[c, k], gcrv.at[me_h], 21, "head", to)
+
+        def step_s(r, z):
+            c = lax.rem(chip + r, CHIPS)
+            use_chunk(c)
+            if h == 1:
+                send_gc(c, 0, 2 * c)
+                send_gc(c, 1, 2 * c + 1)
             return z
 
-        lax.fori_loop(0, CH, step_s, 0)
-
+        lax.fori_loop(1, CHIPS, step_s, 0)
+        use_chunk(chip)
+        if h == 1:
+            send_gc(chip, 1 - core, sibling)
+            local(gcb.at[chip, core], gcrv.at[me_h], 21)
+
+    def pair_sums(h):
+        half = half_of(h)
+        gi, si = gin[:, half].astype(F32), sin[:, half].astype(F32)
+        for c in range(CH):
+            ge = lg[c, :, half] + rowf[2 * CH + c : 2 * CH + c + 1, half] * gi
+            se = ls[c + 1, :, half] + rowf[CH + c : CH + c + 1, half] * si
+            prod[c : c + 1, half] = jnp.sum(ge * se, axis=0, keepdims=True)
+        prod[CH : CH + 1, half] = jnp.sum(gi * si, axis=0, keepdims=True)
+
+    prod[...] = jnp.zeros_like(prod)
     use_s(0)
+    pair_sums(0)
     arrived(gbo, 19)
     gbh[...] = gbp[:, pl.ds(core, 1)].reshape(CHIPS, TOK, N) + gbo[...]
 
@@ -446,29 +473,16 @@
 
     use_s(1)
 
-    def send_gc(r, z):
-        to = hpeer(r)
-        remote(gcb.at[to // 2, lax.rem(to, 2)], gcrv.at[me_h], 21, "head", to)
-        return z
-
-    lax.fori_loop(1, NH, send_gc, 0)
-    local(gcb.at[chip, core], gcrv.at[me_h], 21)
-
+    pair_sums(1)
     arrived(pairr, 16)
-    gi, si = gin[...].astype(F32), sin[...].astype(F32)
     exact = []
     for h in range(2):
         for a in range(LG):
             exact.append(jnp.sum(pairr[a * RG : (a + 1) * RG, h], axis=0))
     fix = rowf[2 * CH - 1 : 2 * CH, :] * (
-        jnp.concatenate(exact, axis=1) - jnp.sum(gi * si, axis=0, keepdims=True)
+        jnp.concatenate(exact, axis=1) - prod[CH : CH + 1, :]
     )
-    prod[...] = jnp.zeros_like(prod)
-    for c in range(CH):
-        ge = lg[c] + rowf[2 * CH + c : 2 * CH + c + 1, :] * gi
-        se = ls[c + 1] + rowf[CH + c : CH + c + 1, :] * si
-        prod[c : c + 1, :] = jnp.sum(ge * se, axis=0, keepdims=True) + fix
-    base = heads_sum(prod[...])
+    base = heads_sum(prod[...] + fix)
     lane = iota((Q, N), 1)
     upper = ones_where(above)
     packed = jnp.zeros((2 * TOK, N), F32)

time: 65.1 us -> 63.8 us (0.980)
  Pallas kernels: 64.2 us -> 62.9 us
    pallas_call x1, Pallas kernels: 62.6 us -> 61.3 us  [body(): pl.pallas_call(kernel, out_shape=(vm((TOK, NH * W), BF), vm((N, 2 * TOK),...]
where the time goes in v4:
time: 63.8 us; the launch traced here: 63.6 us
  Pallas kernels  62.9 us (99%)
  between operations  0.64 us (1%)
    pallas_call x1, Pallas kernels, body(): pl.pallas_call(kernel, out_shape=(vm((TOK, NH * W), BF), vm((N, 2 * TOK),...  61.3 us
    pallas_call x1, Pallas kernels, body(): pl.pallas_call(finish, out_shape=(jax.ShapeDtypeStruct((TOK, NH * W), BF)...  1.62 us

profile of v4, /device:TPU:1, one launch (start us, length us, event | category | flops | bytes accessed | tf_op | source)
XLA Modules:
  0.0 63.6 jit_solution(11908529481578052532)
XLA Ops:
  0.6 61.3 %block_backward.1 = (bf16[64,8192]{1,0:T(8,128)(2,1)S(1)}, bf16[128,128]{1,0:T(8,128)(2,1)S(1)}, f32[4,64,128]{2,1,0:T(8,128)S(1)}, bf16[8,64,128]{2,1,0:T(8,128)(2,1)S(1)}) custom-call(bf16[64,8192]{1,0:T(8,128)(2,1)} %x.1, bf16[64,8192]{1,0:T(8,128)(2,1)} %g.1, bf16[64,128]{1,0:T(8,128)(2,1)} %st.1, bf16[64,128]{1,0:T(8,128)(2,1)} %ld.1, ...), custom_call_target="tpu_custom_call" | custom-call | flops 3000000000 | bytes 8388608 | tf_op jit(solution)/shard_map/block_backward/pallas_call | solution.py:552
  62.0 1.6 %finish.1 = (bf16[64,8192]{1,0:T(8,128)(2,1)}, bf16[64,128]{1,0:T(8,128)(2,1)}, bf16[64,128]{1,0:T(8,128)(2,1)}, f32[64,128]{1,0:T(8,128)}, f32[64,128]{1,0:T(8,128)}) custom-call(bf16[64,8192]{1,0:T(8,128)(2,1)S(1)} %get-tuple-element.9.ox, bf16[128,128]{1,0:T(8,128)(2,1)S(1)} %get-tuple-element.10.pkv, f32[4,64,128]{2,1,0:T(8,128)S(1)} %get-tuple-element.11.gbrv, ...), custom_call_target="tpu_custom_call" | custom-call | flops 1048576 | bytes 3145728 | tf_op jit(solution)/shard_map/finish/pallas_call | solution.py:623

commit v5 on v4

--- a/solution.py
+++ b/solution.py
@@ -23,6 +23,8 @@
 RG = N // RB
 LG = HW // N
 CHIPS = NH // 2
+Z = 8
+FAR_FIRST = sorted(range(1, NC), key=lambda r: (-min(r % Z, Z - r % Z), r))
 EARLY = 1
 
 NN = ((1,), (0,))
@@ -247,12 +249,9 @@
             dst[a : a + RB, b : b + N] = src[h, k]
 
     def spread(src, dst, s, h):
-        def one(r, z):
+        for r in FAR_FIRST:
             k = cpeer(r)
             remote(src.at[h, k], dst.at[h, me_c], s + h, "ctx", k)
-            return z
-
-        lax.fori_loop(1, NC, one, 0)
         local(src.at[h, me_c], dst.at[h, me_c], s + h)
 
     def half_of(h):
@@ -461,7 +460,7 @@
     use_s(0)
     pair_sums(0)
     arrived(gbo, 19)
-    gbh[...] = gbp[:, pl.ds(core, 1)].reshape(CHIPS, TOK, N) + gbo[...]
+    gbh[...] = (gbp[:, pl.ds(core, 1)].reshape(CHIPS, TOK, N) + gbo[...]).astype(BF)
 
     def send_gb(r, z):
         p = lax.rem(chip + r, CHIPS)
@@ -537,7 +536,7 @@
     back = jnp.transpose(pkv[...].astype(F32)).astype(BF)
     ods[...] = back[0:TOK, :]
     odq[...] = back[TOK:, :]
-    ogb[...] = jnp.sum(gbrv[...], axis=0)
+    ogb[...] = jnp.sum(gbrv[...].astype(F32), axis=0)
     ogc[...] = jnp.sum(gcrv[...].astype(F32), axis=0)
     move.wait()
 
@@ -554,7 +553,7 @@
         out_shape=(
             vm((TOK, NH * W), BF),
             vm((N, 2 * TOK), BF),
-            vm((CHIPS, TOK, N), F32),
+            vm((CHIPS, TOK, N), BF),
             vm((NH, TOK, N), BF),
         ),
         in_specs=[hbm] * 6 + [vmem],
@@ -605,7 +604,7 @@
             vm((CHIPS, 2, TOK, N), F32),
             vm((CHIPS, 2, TOK, N), F32),
             vm((CHIPS, TOK, N), F32),
-            vm((CHIPS, TOK, N), F32),
+            vm((CHIPS, TOK, N), BF),
             vm((CHIPS, 2, TOK, N), BF),
             vm((N, 2 * TOK), BF),
             pltpu.SemaphoreType.DMA((24,)),

time: 63.8 us -> 63.1 us (0.989)
  Pallas kernels: 62.9 us -> 62.2 us
    pallas_call x1, Pallas kernels: 61.3 us -> 60.5 us  [body(): pl.pallas_call(kernel, out_shape=(vm((TOK, NH * W), BF), vm((N, 2 * TOK),...]
where the time goes in v5:
time: 63.1 us; the launch traced here: 62.8 us
  Pallas kernels  62.2 us (99%)
  between operations  0.64 us (1%)
    pallas_call x1, Pallas kernels, body(): pl.pallas_call(kernel, out_shape=(vm((TOK, NH * W), BF), vm((N, 2 * TOK),...  60.5 us
    pallas_call x1, Pallas kernels, body(): pl.pallas_call(finish, out_shape=(jax.ShapeDtypeStruct((TOK, NH * W), BF)...  1.62 us

profile of v5, /device:TPU:1, one launch (start us, length us, event | category | flops | bytes accessed | tf_op | source)
XLA Modules:
  0.0 62.8 jit_solution(5510561036715241298)
XLA Ops:
  0.6 60.5 %block_backward.1 = (bf16[64,8192]{1,0:T(8,128)(2,1)S(1)}, bf16[128,128]{1,0:T(8,128)(2,1)S(1)}, bf16[4,64,128]{2,1,0:T(8,128)(2,1)S(1)}, bf16[8,64,128]{2,1,0:T(8,128)(2,1)S(1)}) custom-call(bf16[64,8192]{1,0:T(8,128)(2,1)} %x.1, bf16[64,8192]{1,0:T(8,128)(2,1)} %g.1, bf16[64,128]{1,0:T(8,128)(2,1)} %st.1, bf16[64,128]{1,0:T(8,128)(2,1)} %ld.1, ...), custom_call_target="tpu_custom_call" | custom-call | flops 3000000000 | bytes 8388608 | tf_op jit(solution)/shard_map/block_backward/pallas_call | solution.py:551
  61.2 1.6 %finish.1 = (bf16[64,8192]{1,0:T(8,128)(2,1)}, bf16[64,128]{1,0:T(8,128)(2,1)}, bf16[64,128]{1,0:T(8,128)(2,1)}, f32[64,128]{1,0:T(8,128)}, f32[64,128]{1,0:T(8,128)}) custom-call(bf16[64,8192]{1,0:T(8,128)(2,1)S(1)} %get-tuple-element.9.ox, bf16[128,128]{1,0:T(8,128)(2,1)S(1)} %get-tuple-element.10.pkv, bf16[4,64,128]{2,1,0:T(8,128)(2,1)S(1)} %get-tuple-element.11.gbrv, ...), custom_call_target="tpu_custom_call" | custom-call | flops 1048576 | bytes 3145728 | tf_op jit(solution)/shard_map/finish/pallas_call | solution.py:622

commit v6 on v5

--- a/solution.py
+++ b/solution.py
@@ -395,8 +395,8 @@
     local_u(1)
     owners_g(1)
     local_x(0)
+    local_x(1)
     channels(0)
-    local_x(1)
     channels(1)
     lax.fori_loop(0, EARLY, step_local, 0)
     owners_s(0)
@@ -418,7 +418,7 @@
         arrived(sbr.at[h], 14 + h)
         unstage(sbr, sin, h)
 
-        def use_chunk(c):
+        def use_chunk(c, leave):
             at = chunk(c)
             gd = gb[at, half].astype(F32) * f1d[at, half]
             gq = dot(gd.astype(BF), sin[:, half], NT)
@@ -428,24 +428,27 @@
                     gcp[c, k] = now
                 else:
                     gcb[c, k] = now.astype(BF)
+            if h == 1:
+                leave(c)
             rs[at, :] = rs[at, :] + heads_sum(gd * dot(sm[1, at, :], sin[:, half]), half)
 
         def send_gc(c, k, to):
             remote(gcb.at[c, k], gcrv.at[me_h], 21, "head", to)
 
+        def leave_far(c):
+            send_gc(c, 0, 2 * c)
+            send_gc(c, 1, 2 * c + 1)
+
+        def leave_near(c):
+            send_gc(c, 1 - core, sibling)
+            local(gcb.at[c, core], gcrv.at[me_h], 21)
+
         def step_s(r, z):
-            c = lax.rem(chip + r, CHIPS)
-            use_chunk(c)
-            if h == 1:
-                send_gc(c, 0, 2 * c)
-                send_gc(c, 1, 2 * c + 1)
+            use_chunk(lax.rem(chip + r, CHIPS), leave_far)
             return z
 
         lax.fori_loop(1, CHIPS, step_s, 0)
-        use_chunk(chip)
-        if h == 1:
-            send_gc(chip, 1 - core, sibling)
-            local(gcb.at[chip, core], gcrv.at[me_h], 21)
+        use_chunk(chip, leave_near)
 
     def pair_sums(h):
         half = half_of(h)

time: 63.1 us -> 63.4 us (level)
  no operation moved by 1% of the time
where the time goes in v6:
time: 63.4 us; the launch traced here: 63.1 us
  Pallas kernels  62.4 us (98%)
  between operations  0.64 us (1%)
    pallas_call x1, Pallas kernels, body(): pl.pallas_call(kernel, out_shape=(vm((TOK, NH * W), BF), vm((N, 2 * TOK),...  60.8 us
    pallas_call x1, Pallas kernels, body(): pl.pallas_call(finish, out_shape=(jax.ShapeDtypeStruct((TOK, NH * W), BF)...  1.62 us

profile of v6, /device:TPU:1, one launch (start us, length us, event | category | flops | bytes accessed | tf_op | source)
XLA Modules:
  0.0 63.1 jit_solution(2540058456125110751)
XLA Ops:
  0.6 60.8 %block_backward.1 = (bf16[64,8192]{1,0:T(8,128)(2,1)S(1)}, bf16[128,128]{1,0:T(8,128)(2,1)S(1)}, bf16[4,64,128]{2,1,0:T(8,128)(2,1)S(1)}, bf16[8,64,128]{2,1,0:T(8,128)(2,1)S(1)}) custom-call(bf16[64,8192]{1,0:T(8,128)(2,1)} %x.1, bf16[64,8192]{1,0:T(8,128)(2,1)} %g.1, bf16[64,128]{1,0:T(8,128)(2,1)} %st.1, bf16[64,128]{1,0:T(8,128)(2,1)} %ld.1, ...), custom_call_target="tpu_custom_call" | custom-call | flops 3000000000 | bytes 8388608 | tf_op jit(solution)/shard_map/block_backward/pallas_call | solution.py:554
  61.5 1.6 %finish.1 = (bf16[64,8192]{1,0:T(8,128)(2,1)}, bf16[64,128]{1,0:T(8,128)(2,1)}, bf16[64,128]{1,0:T(8,128)(2,1)}, f32[64,128]{1,0:T(8,128)}, f32[64,128]{1,0:T(8,128)}) custom-call(bf16[64,8192]{1,0:T(8,128)(2,1)S(1)} %get-tuple-element.9.ox, bf16[128,128]{1,0:T(8,128)(2,1)S(1)} %get-tuple-element.10.pkv, bf16[4,64,128]{2,1,0:T(8,128)(2,1)S(1)} %get-tuple-element.11.gbrv, ...), custom_call_target="tpu_custom_call" | custom-call | flops 1048576 | bytes 3145728 | tf_op jit(solution)/shard_map/finish/pallas_call | solution.py:625
